TPU v7x, 128 devices: a whole 4x4x4 slice. The times are simulated.
128 devices in a mesh: row: 16 (over y_lo, z, core), col: 8 (over y_hi, x).
Axes of the slice: x: 4, y: 4 (y_hi: 2, y_lo: 2; y = y_hi * 2 + y_lo), z: 4, core: 2. Of those that a mesh axis runs over, the one named last changes fastest.
Arguments:
- tokens: bfloat16 [1024, 6144], P('col', 'row'), may hold values from -6 to 6
- weight_in: bfloat16 [6144, 24576], P('row', 'col'), may hold values from -0.078125 to 0.078125
- weight_out: bfloat16 [24576, 6144], P('col', 'row'), may hold values from -0.078125 to 0.078125
- upstream: bfloat16 [1024, 6144], P('col', 'row'), may hold values from -6 to 6
Outputs:
- grad_tokens: bfloat16 [1024, 6144], P('col', 'row')
- grad_in: bfloat16 [6144, 24576], P('row', 'col')
- grad_out: bfloat16 [24576, 6144], P('col', 'row')
All inputs are finite; a program needn't handle non-finite values.
Results may differ from a plain program's by a relative error of at most 0.005.
Values may be sent and summed in bfloat16 or wider, within the bound.
A program may use at most 128 MiB of HBM per device.

v0:
```python
import jax
import jax.numpy as jnp
from jax import lax
from jax.sharding import PartitionSpec as P

coef = 0.7978845608
cubic = 0.044715


def activate(hidden, back):
    inner = coef * (hidden + cubic * hidden * hidden * hidden)
    tangent = jnp.tanh(inner)
    value = 0.5 * hidden * (1.0 + tangent)
    slope = 0.5 * (1.0 + tangent) + 0.5 * hidden * (1.0 - tangent * tangent) * coef * (
        1.0 + 3.0 * cubic * hidden * hidden
    )
    return (value.astype(jnp.bfloat16), (back * slope).astype(jnp.bfloat16))


def contract_last(left, right):
    return lax.dot_general(
        left, right, (((1,), (1,)), ((), ())), preferred_element_type=jnp.float32
    )


def contract_first(left, right):
    return lax.dot_general(
        left, right, (((0,), (0,)), ((), ())), preferred_element_type=jnp.float32
    )


def shards(tokens, weight_in, weight_out, upstream):
    tok_all, cot_all = (
        lax.all_gather(tokens, "col", axis=0, tiled=True),
        lax.all_gather(upstream, "col", axis=0, tiled=True),
    )
    width_hid = weight_in.shape[1]
    sums = lax.psum_scatter(
        jnp.concatenate(
            [
                jnp.dot(tok_all, weight_in, preferred_element_type=jnp.float32),
                contract_last(cot_all, weight_out),
            ],
            axis=1,
        ),
        "row",
        scatter_dimension=0,
        tiled=True,
    )
    hidden_local = sums[:, :width_hid]
    back_local = sums[:, width_hid:]
    act_local, grad_local = activate(hidden_local, back_local)
    act_all, grad_all = (
        lax.all_gather(act_local, "row", axis=0, tiled=True),
        lax.all_gather(grad_local, "row", axis=0, tiled=True),
    )
    grad_in = contract_first(tok_all, grad_all).astype(jnp.bfloat16)
    grad_out = contract_first(act_all, cot_all).astype(jnp.bfloat16)
    grad_tokens = lax.psum_scatter(
        contract_last(grad_all, weight_in), "col", scatter_dimension=0, tiled=True
    ).astype(jnp.bfloat16)
    return (grad_tokens, grad_in, grad_out)


def solution(mesh):
    placed = (P("col", "row"), P("row", "col"), P("col", "row"), P("col", "row"))
    return jax.shard_map(
        shards,
        mesh=mesh,
        in_specs=placed,
        out_specs=(P("col", "row"), P("row", "col"), P("col", "row")),
        check_vma=False,
    )
```

profile of v0, /device:TPU:0, one launch (start us, length us, event | category | flops | bytes accessed | tf_op | source)
XLA Modules:
  0.0 416.0 jit_solution(14746245070475281897)
XLA Ops:
  7.2 0.0 copy-start
  7.2 0.0 reduce-scatter.3.cloned.1.call-start
  7.2 36.7 %all_gather.12 = bf16[1024,384]{1,0:T(8,128)(2,1)S(1)} all-gather(bf16[128,384]{1,0:T(8,128)(2,1)} %param.4), channel_id=1, replica_groups=mesh['row'=16,'col'=8] {'col'}, dimensions={0}, use_global_device_ids=true | all-gather | bytes 884736 | tf_op jit(solution)/shard_map/all_gather | solution.py:34
  43.9 35.8 %all_gather.13 = bf16[1024,384]{1,0:T(8,128)(2,1)S(1)} all-gather(bf16[128,384]{1,0:T(8,128)(2,1)} %param.7), channel_id=1, replica_groups=mesh['row'=16,'col'=8] {'col'}, dimensions={0}, use_global_device_ids=true | all-gather | bytes 884736 | tf_op jit(solution)/shard_map/all_gather | solution.py:35
  79.7 5.4 %fusion.9 = f32[1024,3072]{1,0:T(8,128)S(1)} fusion(bf16[1024,384]{1,0:T(8,128)(2,1)S(1)} %all_gather.13, bf16[3072,384]{1,0:T(8,128)(2,1)} %param.6), kind=kOutput, calls=%fused_computation.15 | convolution fusion | flops 2415919104 | bytes 15728640 | tf_op jit(solution)/shard_map/dot_general | solution.py:21
  85.2 3.4 fusion.8
  88.6 8.7 %pad_maximum_fusion = f32[1024,6144]{1,0:T(8,128)} fusion(f32[1024,3072]{1,0:T(8,128)S(1)} %fusion.9, f32[1024,3072]{1,0:T(8,128)S(1)} %fusion.8), kind=kLoop, calls=%fused_computation | loop fusion | flops 6291456 | bytes 50331648 | tf_op jit(solution)/shard_map/concatenate | solution.py:39
  97.3 0.0 reduce-scatter.3.cloned.1.call-update
  97.4 0.0 all-gather.3.cloned.1.call-start
  97.4 142.9 %reduce-scatter.3.cloned.1.call-done = f32[64,6144]{1,0:T(8,128)} async-done(((f32[1024,6144]{1,0:T(8,128)}), f32[64,6144]{1,0:T(8,128)}) %reduce-scatter.3.cloned.1.call-update) | async-done | bytes 1572880 | tf_op jit(solution)/shard_map/reduce_scatter | solution.py:38
  240.3 2.8 multiply_convert_fusion
  243.0 0.0 all-gather.3.cloned.1.call-update
  243.1 0.0 all-gather.5.cloned.1.call-start
  243.1 0.7 all-gather.5.cloned.1.call-update
  243.8 0.2 reduce-scatter.5.cloned.1.call-start
  244.0 40.1 %all-gather.3.cloned.1.call-done = bf16[1024,3072]{1,0:T(8,128)(2,1)} async-done(((bf16[64,3072]{1,0:T(8,128)(2,1)}), bf16[1024,3072]{1,0:T(8,128)(2,1)}) %all-gather.3.cloned.1.call-update) | async-done | bytes 6291472 | tf_op jit(solution)/shard_map/all_gather | solution.py:55
  284.2 6.7 %fusion.10 = f32[1024,384]{1,0:T(8,128)} fusion(bf16[1024,3072]{1,0:T(8,128)(2,1)} %all-gather.3.cloned.1.call-done, bf16[384,3072]{1,0:T(8,128)(2,1)S(1)} %copy-done), kind=kOutput, calls=%fused_computation.16 | convolution fusion | flops 2415919104 | bytes 10223616 | tf_op jit(solution)/shard_map/dot_general | solution.py:21
  290.8 0.0 reduce-scatter.5.cloned.1.call-update
  290.9 7.7 %fusion = bf16[384,3072]{0,1:T(8,128)(2,1)} fusion(bf16[1024,3072]{1,0:T(8,128)(2,1)} %all-gather.3.cloned.1.call-done, bf16[1024,384]{1,0:T(8,128)(2,1)S(1)} %all_gather.12), kind=kOutput, calls=%fused_computation.3 | convolution fusion | flops 2417098752 | bytes 9437184 | tf_op jit(solution)/shard_map/dot_general | solution.py:27
  298.5 4.3 %copy.7 = bf16[384,3072]{1,0:T(8,128)(2,1)} copy(bf16[384,3072]{0,1:T(8,128)(2,1)} %fusion) | data formatting | bytes 4718592
  302.9 26.3 %all-gather.5.cloned.1.call-done = bf16[1024,3072]{1,0:T(8,128)(2,1)} async-done(((bf16[64,3072]{1,0:T(8,128)(2,1)}), bf16[1024,3072]{1,0:T(8,128)(2,1)}) %all-gather.5.cloned.1.call-update) | async-done | bytes 6291472 | tf_op jit(solution)/shard_map/all_gather | solution.py:54
  329.2 7.7 %convolution_convert_fusion = bf16[3072,384]{1,0:T(8,128)(2,1)} fusion(bf16[1024,3072]{1,0:T(8,128)(2,1)} %all-gather.5.cloned.1.call-done, bf16[1024,384]{1,0:T(8,128)(2,1)S(1)} %copy-done.2), kind=kOutput, calls=%fused_computation.1 | convolution fusion | flops 2417098752 | bytes 9437184 | tf_op jit(solution)/shard_map/dot_general | solution.py:27
  336.8 71.0 %reduce-scatter.5.cloned.1.call-done = f32[128,384]{1,0:T(8,128)} async-done(((f32[1024,384]{1,0:T(8,128)}), f32[128,384]{1,0:T(8,128)}) %reduce-scatter.5.cloned.1.call-update) | async-done | bytes 196624 | tf_op jit(solution)/shard_map/reduce_scatter | solution.py:59
  407.9 1.6 convert_element_type.19
  (5 shorter events, 0.0 us)
Async XLA Ops:
  7.2 78.0 %copy-start = (bf16[384,3072]{1,0:T(8,128)(2,1)S(1)}, bf16[384,3072]{1,0:T(8,128)(2,1)}, u32[]{:S(2)}) copy-start(bf16[384,3072]{1,0:T(8,128)(2,1)} %param.5) | copy-start | bytes 7077892
  7.2 233.1 %reduce-scatter.3.cloned.1.call-start = ((), (), s32[]{:S(2)}) async-start(), calls=%async_computation.2 | async-start | bytes 26738688 | tf_op jit(solution)/shard_map/reduce_scatter | solution.py:38
  79.7 5.4 %copy-start.1 = (bf16[1024,384]{1,0:T(8,128)(2,1)}, bf16[1024,384]{1,0:T(8,128)(2,1)S(1)}, u32[]{:S(2)}) copy-start(bf16[1024,384]{1,0:T(8,128)(2,1)S(1)} %all_gather.13) | copy-start | bytes 2359300
  97.4 186.8 %all-gather.3.cloned.1.call-start = ((), (), s32[]{:S(2)}) async-start(), calls=%async_computation.3 | async-start | bytes 6684672 | tf_op jit(solution)/shard_map/all_gather | solution.py:55
  243.1 86.1 %all-gather.5.cloned.1.call-start = ((), (), s32[]{:S(2)}) async-start(), calls=%async_computation.5 | async-start | bytes 6684672 | tf_op jit(solution)/shard_map/all_gather | solution.py:54
  243.8 164.1 %reduce-scatter.5.cloned.1.call-start = ((), (), s32[]{:S(2)}) async-start(), calls=%async_computation.4 | async-start | bytes 1769472 | tf_op jit(solution)/shard_map/reduce_scatter | solution.py:59
  298.5 30.6 %copy-start.2 = (bf16[1024,384]{1,0:T(8,128)(2,1)S(1)}, bf16[1024,384]{1,0:T(8,128)(2,1)}, u32[]{:S(2)}) copy-start(bf16[1024,384]{1,0:T(8,128)(2,1)} %copy-done.1) | copy-start | bytes 2359300
Sparse Core Ops, SparseCore 0:
  97.5 142.7 reduce-scatter.2
  243.2 40.9 all-gather.2
  285.9 43.2 all-gather.4
  332.8 75.0 reduce-scatter.4
where the time goes:
time: 416 us
  waiting for transfers between devices  281 us (68%)
  blocking collectives  72.5 us (17%)
  matrix products  30.9 us (7%)
  between operations  13.8 us (3%)
  other arithmetic  13.1 us (3%)
  local copies, waits for them, and re-layouts  4.37 us (1%)
    reduce_scatter x1, waiting for transfers between devices, shards(): lax.psum_scatter(jnp.concatenate([jnp.dot(tok_all, weight_in, preferred_e...  143 us
    reduce_scatter x1, waiting for transfers between devices, shards(): lax.psum_scatter(contract_last(grad_all, weight_in), 'col', scatter_dimen...  71 us
    all_gather x1, waiting for transfers between devices, shards(): lax.all_gather(grad_local, 'row', axis=0, tiled=True)  40.1 us
    all_gather x1, blocking collectives, shards(): lax.all_gather(tokens, 'col', axis=0, tiled=True)  36.7 us
    all_gather x1, blocking collectives, shards(): lax.all_gather(upstream, 'col', axis=0, tiled=True)  35.8 us
    all_gather x1, waiting for transfers between devices, shards(): lax.all_gather(act_local, 'row', axis=0, tiled=True)  26.3 us
    dot_general x2, matrix products, contract_first(): lax.dot_general(left, right, (((0,), (0,)), ((), ())), preferred_element_...  15.3 us
    dot_general x2, matrix products, contract_last(): lax.dot_general(left, right, (((1,), (1,)), ((), ())), preferred_element_...  12.1 us
  transfers between devices with their start and end apart: 4, of which 4 were waited for; matrix products, arithmetic and copies ran while one was open for 6% of the time, Pallas kernels for 0%

commit v1 on v0

--- a/solution.py
+++ b/solution.py
@@ -5,6 +5,15 @@
 
 coef = 0.7978845608
 cubic = 0.044715
+cover_stacks_all_by_axis = lambda m: jnp.concatenate(
+    lax.all_to_all(
+        jnp.stack([m for _ in range(lax.axis_size("row"))]),
+        axis_name="row",
+        split_axis=0,
+        concat_axis=0,
+    ),
+    0,
+)
 
 
 def activate(hidden, back):
@@ -51,7 +60,7 @@
     back_local = sums[:, width_hid:]
     act_local, grad_local = activate(hidden_local, back_local)
     act_all, grad_all = (
-        lax.all_gather(act_local, "row", axis=0, tiled=True),
+        cover_stacks_all_by_axis(act_local),
         lax.all_gather(grad_local, "row", axis=0, tiled=True),
     )
     grad_in = contract_first(tok_all, grad_all).astype(jnp.bfloat16)

time: 416 us -> 454 us (1.091)
  waiting for transfers between devices: 281 us -> 310 us
  starting transfers between devices: 0.34 us -> 4.93 us
    all_gather x1, waiting for transfers between devices: 40.1 us -> 103 us  [shards(): lax.all_gather(grad_local, 'row', axis=0, tiled=True)]
    all_gather x1 -> x0, waiting for transfers between devices: 26.3 us -> none  [shards(): lax.all_gather(act_local, 'row', axis=0, tiled=True)]
    reduce_scatter x1, waiting for transfers between devices: 71 us -> 62.7 us  [shards(): lax.psum_scatter(contract_last(grad_all, weight_in), 'col', scatter_dimen...]
    all_to_all x0 -> x1, starting transfers between devices: none -> 4.63 us  [lax.all_to_all(jnp.stack([m for _ in range(lax.axis_size('row'))]), axis_...]
  transfers between devices with their start and end apart: 4 -> 4, of which waited for: 4 -> 4; matrix products, arithmetic and copies ran while one was open for 6% -> 7% of each run, Pallas kernels for 0% -> 0%
where the time goes in v1:
time: 454 us; the launch traced here: 453 us
  waiting for transfers between devices  310 us (68%)
  blocking collectives  72.5 us (16%)
  matrix products  30.8 us (7%)
  between operations  13.8 us (3%)
  other arithmetic  13 us (3%)
  local copies, waits for them, and re-layouts  8.56 us (2%)
  starting transfers between devices  4.93 us (1%)
    reduce_scatter x1, waiting for transfers between devices, shards(): lax.psum_scatter(jnp.concatenate([jnp.dot(tok_all, weight_in, preferred_e...  143 us
    all_gather x1, waiting for transfers between devices, shards(): lax.all_gather(grad_local, 'row', axis=0, tiled=True)  103 us
    reduce_scatter x1, waiting for transfers between devices, shards(): lax.psum_scatter(contract_last(grad_all, weight_in), 'col', scatter_dimen...  62.7 us
    all_gather x1, blocking collectives, shards(): lax.all_gather(tokens, 'col', axis=0, tiled=True)  36.7 us
    all_gather x1, blocking collectives, shards(): lax.all_gather(upstream, 'col', axis=0, tiled=True)  35.8 us
    dot_general x2, matrix products, contract_first(): lax.dot_general(left, right, (((0,), (0,)), ((), ())), preferred_element_...  15.5 us
    dot_general x2, matrix products, contract_last(): lax.dot_general(left, right, (((1,), (1,)), ((), ())), preferred_element_...  11.8 us
  transfers between devices with their start and end apart: 4, of which 4 were waited for; matrix products, arithmetic and copies ran while one was open for 7% of the time, Pallas kernels for 0%

profile of v1, /device:TPU:0, one launch (start us, length us, event | category | flops | bytes accessed | tf_op | source)
XLA Modules:
  0.0 453.1 jit_solution(4543105276841453667)
XLA Ops:
  7.2 0.0 reduce-scatter.3.cloned.1.call-start
  7.2 36.7 %all_gather.9 = bf16[1024,384]{1,0:T(8,128)(2,1)S(1)} all-gather(bf16[128,384]{1,0:T(8,128)(2,1)} %param.4), channel_id=1, replica_groups=mesh['row'=16,'col'=8] {'col'}, dimensions={0}, use_global_device_ids=true | all-gather | bytes 884736 | tf_op jit(solution)/shard_map/all_gather | solution.py:43
  43.9 35.8 %all_gather.10 = bf16[1024,384]{1,0:T(8,128)(2,1)S(1)} all-gather(bf16[128,384]{1,0:T(8,128)(2,1)} %param.7), channel_id=1, replica_groups=mesh['row'=16,'col'=8] {'col'}, dimensions={0}, use_global_device_ids=true | all-gather | bytes 884736 | tf_op jit(solution)/shard_map/all_gather | solution.py:44
  79.7 0.9 copy-done.1
  80.6 5.1 %fusion.9 = f32[1024,3072]{1,0:T(8,128)S(1)} fusion(bf16[1024,384]{1,0:T(8,128)(2,1)S(1)} %all_gather.10, bf16[3072,384]{1,0:T(8,128)(2,1)} %param.6), kind=kOutput, calls=%fused_computation.15 | convolution fusion | flops 2415919104 | bytes 15728640 | tf_op jit(solution)/shard_map/dot_general | solution.py:30
  85.8 3.4 fusion.8
  89.2 8.7 %pad_maximum_fusion = f32[1024,6144]{1,0:T(8,128)} fusion(f32[1024,3072]{1,0:T(8,128)S(1)} %fusion.9, f32[1024,3072]{1,0:T(8,128)S(1)} %fusion.8), kind=kLoop, calls=%fused_computation | loop fusion | flops 6291456 | bytes 50331648 | tf_op jit(solution)/shard_map/concatenate | solution.py:48
  97.9 0.0 reduce-scatter.3.cloned.1.call-update
  98.0 0.0 all-gather.2.cloned.1.call-start
  98.0 142.8 %reduce-scatter.3.cloned.1.call-done = f32[64,6144]{1,0:T(8,128)} async-done(((f32[1024,6144]{1,0:T(8,128)}), f32[64,6144]{1,0:T(8,128)}) %reduce-scatter.3.cloned.1.call-update) | async-done | bytes 1572880 | tf_op jit(solution)/shard_map/reduce_scatter | solution.py:47
  240.8 2.7 multiply_convert_fusion
  243.5 0.0 all-gather.2.cloned.1.call-update
  243.5 3.4 stack.2
  246.9 4.6 %all-to-all-start = ((bf16[16,64,3072]{2,1,0:T(8,128)(2,1)}), bf16[16,64,3072]{2,1,0:T(8,128)(2,1)}, u32[]{:S(2)}, u32[]{:S(2)}) async-start(bf16[16,64,3072]{2,1,0:T(8,128)(2,1)} %stack.2), calls=%async_computation.2 | async-start | bytes 12582912 | tf_op jit(solution)/shard_map/all_to_all | solution.py:9
  251.5 0.2 reduce-scatter.5.cloned.1.call-start
  251.8 102.9 %all-gather.2.cloned.1.call-done = bf16[1024,3072]{1,0:T(8,128)(2,1)} async-done(((bf16[64,3072]{1,0:T(8,128)(2,1)}), bf16[1024,3072]{1,0:T(8,128)(2,1)}) %all-gather.2.cloned.1.call-update) | async-done | bytes 6291472 | tf_op jit(solution)/shard_map/all_gather | solution.py:64
  354.6 6.7 %fusion.10 = f32[1024,384]{1,0:T(8,128)} fusion(bf16[1024,3072]{1,0:T(8,128)(2,1)} %all-gather.2.cloned.1.call-done, bf16[384,3072]{1,0:T(8,128)(2,1)S(1)} %copy-done), kind=kOutput, calls=%fused_computation.16 | convolution fusion | flops 2415919104 | bytes 10223616 | tf_op jit(solution)/shard_map/dot_general | solution.py:30
  361.3 0.0 reduce-scatter.5.cloned.1.call-update
  361.3 1.2 all-to-all-done
  362.5 7.8 %convolution_convert_fusion = bf16[3072,384]{1,0:T(8,128)(2,1)} fusion(bf16[1024,3072]{1,0:T(8,128)(2,1)} %bitcast.1, bf16[1024,384]{1,0:T(8,128)(2,1)} %copy-done.1), kind=kOutput, calls=%fused_computation.1 | convolution fusion | flops 2417098752 | bytes 9437184 | tf_op jit(solution)/shard_map/dot_general | solution.py:36
  370.4 7.7 %fusion = bf16[384,3072]{0,1:T(8,128)(2,1)} fusion(bf16[1024,3072]{1,0:T(8,128)(2,1)} %all-gather.2.cloned.1.call-done, bf16[1024,384]{1,0:T(8,128)(2,1)S(1)} %all_gather.9), kind=kOutput, calls=%fused_computation.3 | convolution fusion | flops 2417098752 | bytes 9437184 | tf_op jit(solution)/shard_map/dot_general | solution.py:36
  378.1 4.3 copy.7
  382.4 62.7 %reduce-scatter.5.cloned.1.call-done = f32[128,384]{1,0:T(8,128)} async-done(((f32[1024,384]{1,0:T(8,128)}), f32[128,384]{1,0:T(8,128)}) %reduce-scatter.5.cloned.1.call-update) | async-done | bytes 196624 | tf_op jit(solution)/shard_map/reduce_scatter | solution.py:68
  445.0 1.6 convert_element_type.19
  (3 shorter events, 0.0 us)
Async XLA Ops:
  7.2 78.6 %copy-start = (bf16[384,3072]{1,0:T(8,128)(2,1)S(1)}, bf16[384,3072]{1,0:T(8,128)(2,1)}, u32[]{:S(2)}) copy-start(bf16[384,3072]{1,0:T(8,128)(2,1)} %param.5) | copy-start | bytes 7077892
  7.2 233.7 %reduce-scatter.3.cloned.1.call-start = ((), (), s32[]{:S(2)}) async-start(), calls=%async_computation.3 | async-start | bytes 26738688 | tf_op jit(solution)/shard_map/reduce_scatter | solution.py:47
  79.7 0.9 copy-start.1
  98.0 256.7 %all-gather.2.cloned.1.call-start = ((), (), s32[]{:S(2)}) async-start(), calls=%async_computation.4 | async-start | bytes 6684672 | tf_op jit(solution)/shard_map/all_gather | solution.py:64
  246.9 115.6 %all-to-all-start = ((bf16[16,64,3072]{2,1,0:T(8,128)(2,1)}), bf16[16,64,3072]{2,1,0:T(8,128)(2,1)}, u32[]{:S(2)}, u32[]{:S(2)}) async-start(bf16[16,64,3072]{2,1,0:T(8,128)(2,1)} %stack.2), calls=%async_computation.2 | async-start | bytes 12582912 | tf_op jit(solution)/shard_map/all_to_all | solution.py:9
  251.5 193.5 %reduce-scatter.5.cloned.1.call-start = ((), (), s32[]{:S(2)}) async-start(), calls=%async_computation.5 | async-start | bytes 1769472 | tf_op jit(solution)/shard_map/reduce_scatter | solution.py:68
Sparse Core Ops, SparseCore 0:
  98.1 142.7 reduce-scatter.2
  243.6 110.9 all-gather.1
  361.4 83.5 reduce-scatter.4
